TPU v7x, 32 devices: a whole 2x2x4 slice. The times are simulated.
32 devices in a mesh: wide: 8 (over z, y), narrow: 4 (over x, core).
Axes of the slice: x: 2, y: 2, z: 4, core: 2. Of those that a mesh axis runs over, the one named last changes fastest.
Arguments:
- slab: bfloat16 [6144, 2048], P('wide', 'narrow'), may hold values from -1.1953125 to 1.1953125
- occupation: float32 [4096], replicated, may hold values from 0.02 to 2
- column_band: int32 [2048], P('narrow'), may hold values from 0 to 4095
- pattern: int32 [48, 12], P('wide'), may hold values from 0 to 47, as said below
Outputs:
- density: bfloat16 [48, 12, 128, 128], P('wide', 'narrow')
Inputs may be any that keep to these rules, and one draw needn't show every extreme that they name: `pattern`: each row c lists 12 different clusters, each equal to (c + d) mod 48 with -8 <= d <= 8; d = -8 and d = 8 appear in every row.
All inputs are finite; a program needn't handle non-finite values.
Results may differ from a plain program's by a relative error of at most 0.015.
Values may be sent and summed in bfloat16 or wider, within the bound.
No kernel may reach another device: no remote copies, remote signals or barrier semaphores. Data moves between devices by JAX's collectives and lax.ppermute only.
A program may use at most 64 MiB of HBM per device.

v0:
```python
import jax
import jax.numpy as jnp
from jax import lax
from jax.sharding import PartitionSpec as P

B = 128
REACH = 8


def from_behind(value, axis, steps):
    count = lax.axis_size(axis)
    pairs = [(source, (source + steps) % count) for source in range(count)]
    return lax.ppermute(value, axis, pairs)


def fetch_rows(slab, steps):
    return from_behind(slab, "wide", steps)


def per_device(slab, occupation, column_band, pattern):
    cl_dev = slab.shape[0] // B
    local_cols = slab.shape[1]
    hops = -(-REACH // cl_dev)
    clusters = cl_dev * lax.axis_size("wide")
    picks = column_band[:, None] == jnp.arange(occupation.shape[0], dtype=jnp.int32)[None, :]
    weight = jnp.sum(jnp.where(picks, occupation[None, :], jnp.float32(0.0)), axis=1)
    scaled = (slab.astype(jnp.float32) * weight[None, :]).astype(jnp.bfloat16)
    pieces = []
    for steps in range(hops, 0, -1):
        pieces.append(fetch_rows(slab, steps))
    pieces.append(slab)
    for steps in range(1, hops + 1):
        pieces.append(fetch_rows(slab, -steps))
    window = jnp.concatenate(pieces, axis=0).reshape(-1, B, local_cols)
    first = lax.axis_index("wide") * cl_dev - hops * cl_dev
    local_index = jnp.mod(pattern - first, clusters)
    right = jnp.take(window, local_index.reshape(-1), axis=0).reshape(
        cl_dev, pattern.shape[1], B, local_cols
    )
    left = scaled.reshape(cl_dev, B, local_cols)
    partial_blocks = jnp.einsum("rik,rnjk->rnij", left, right, preferred_element_type=jnp.float32)
    summed = lax.psum(partial_blocks.astype(jnp.bfloat16), "narrow").astype(jnp.float32)
    share = pattern.shape[1] // lax.axis_size("narrow")
    start = lax.axis_index("narrow") * share
    mine = lax.dynamic_slice_in_dim(summed, start, share, 1)
    return mine.astype(jnp.bfloat16)


def solution(mesh):
    placed = (P("wide", "narrow"), P(), P("narrow"), P("wide", None))
    return jax.shard_map(
        per_device,
        mesh=mesh,
        in_specs=placed,
        out_specs=P("wide", "narrow", None, None),
        check_vma=False,
    )
```

profile of v0, /device:TPU:0, one launch (start us, length us, event | category | flops | bytes accessed | tf_op | source)
XLA Modules:
  0.0 148.2 jit_solution(2974798628394374365)
XLA Ops:
  6.5 0.0 copy-start
  6.5 0.0 all-reduce.2.cloned.1.call-start
  6.5 3.0 %collective-permute-start = (bf16[768,512]{1,0:T(8,128)(2,1)}, bf16[768,512]{1,0:T(8,128)(2,1)}, u32[]{:S(2)}, u32[]{:S(2)}) collective-permute-start(bf16[768,512]{1,0:T(8,128)(2,1)} %param.4), channel_id=1, source_target_pairs={{0,8},{4,12},{8,16},{12,20},{16,24},{20,28},{24,0},{28,4},{1,9},{5... | collective-permute-start | bytes 2359304 | tf_op jit(solution)/shard_map/ppermute | solution.py:13
  9.6 1.5 %collective-permute-start.1 = (bf16[768,512]{1,0:T(8,128)(2,1)}, bf16[768,512]{1,0:T(8,128)(2,1)S(1)}, u32[]{:S(2)}, u32[]{:S(2)}) collective-permute-start(bf16[768,512]{1,0:T(8,128)(2,1)} %param.4), channel_id=1, source_target_pairs={{0,4},{4,8},{8,12},{12,16},{16,20},{20,24},{24,28},{28,0},{1,5},{5... | collective-permute-start | bytes 2359304 | tf_op jit(solution)/shard_map/ppermute | solution.py:13
  11.1 3.2 %collective-permute-start.2 = (bf16[768,512]{1,0:T(8,128)(2,1)}, bf16[768,512]{1,0:T(8,128)(2,1)S(1)}, u32[]{:S(2)}, u32[]{:S(2)}) collective-permute-start(bf16[768,512]{1,0:T(8,128)(2,1)} %param.4), channel_id=1, source_target_pairs={{0,28},{4,0},{8,4},{12,8},{16,12},{20,16},{24,20},{28,24},{1,29},{... | collective-permute-start | bytes 2359304 | tf_op jit(solution)/shard_map/ppermute | solution.py:13
  14.3 0.3 collective-permute-start.3
  14.6 1.9 %select_reduce_fusion = f32[512]{0:T(512)S(1)} fusion(f32[4096]{0:T(1024)} %param.5, s32[512]{0:T(512)} %param.6), kind=kLoop, calls=%fused_computation.4 | loop fusion | flops 6290944 | bytes 20480 | tf_op jit(solution)/shard_map/reduce_sum | solution.py:26
  16.5 0.7 compare_and_fusion
  17.2 0.1 reshape.50
  17.3 2.2 %multiply_convert_fusion = bf16[768,512]{1,0:T(8,128)(2,1)} fusion(bf16[768,512]{1,0:T(8,128)(2,1)} %param.4, f32[512]{0:T(512)S(1)} %select_reduce_fusion), kind=kLoop, calls=%fused_computation.8 | loop fusion | flops 1179648 | bytes 1574912 | tf_op jit(solution)/shard_map/convert_element_type | solution.py:27
  19.5 10.9 %collective-permute-done = bf16[768,512]{1,0:T(8,128)(2,1)} collective-permute-done((bf16[768,512]{1,0:T(8,128)(2,1)}, bf16[768,512]{1,0:T(8,128)(2,1)}, u32[]{:S(2)}, u32[]{:S(2)}) %collective-permute-start) | collective-permute-done | bytes 786464 | tf_op jit(solution)/shard_map/ppermute | solution.py:13
  30.4 2.1 %constant_dynamic-update-slice_fusion.4 = bf16[3840,512]{1,0:T(8,128)(2,1)} fusion(bf16[768,512]{1,0:T(8,128)(2,1)} %collective-permute-done), kind=kLoop, calls=%fused_computation.15 | loop fusion | bytes 1572864
  32.4 15.8 %collective-permute-done.1 = bf16[768,512]{1,0:T(8,128)(2,1)S(1)} collective-permute-done((bf16[768,512]{1,0:T(8,128)(2,1)}, bf16[768,512]{1,0:T(8,128)(2,1)S(1)}, u32[]{:S(2)}, u32[]{:S(2)}) %collective-permute-start.1) | collective-permute-done | bytes 786464 | tf_op jit(solution)/shard_map/ppermute | solution.py:13
  48.3 0.9 constant_dynamic-update-slice_fusion.3
  49.2 0.0 copy-done
  49.2 0.9 constant_dynamic-update-slice_fusion.2
  50.2 0.0 collective-permute-done.2
  50.2 0.9 constant_dynamic-update-slice_fusion.1
  51.1 12.0 %collective-permute-done.3 = bf16[768,512]{1,0:T(8,128)(2,1)S(1)} collective-permute-done((bf16[768,512]{1,0:T(8,128)(2,1)}, bf16[768,512]{1,0:T(8,128)(2,1)S(1)}, u32[]{:S(2)}, u32[]{:S(2)}) %collective-permute-start.3) | collective-permute-done | bytes 786464 | tf_op jit(solution)/shard_map/ppermute | solution.py:13
  63.1 1.0 constant_dynamic-update-slice_fusion
  64.1 0.0 copy-start.1
  64.1 8.1 %gather_fusion = bf16[72,128,512]{2,1,0:T(8,128)(2,1)} fusion(bf16[30,128,512]{2,1,0:T(8,128)(2,1)} %bitcast, s32[1024]{0:T(1024)S(1)} %pad_clamp_fusion), kind=kCustom, calls=%fused_computation | custom fusion | bytes 18874656 | tf_op jit(solution)/shard_map/jit(_take)/gather | solution.py:37
  72.2 0.0 copy-done.1
  72.2 7.7 %convert_bitcast_fusion = bf16[6,12,128,128]{2,3,1,0:T(8,128)(2,1)} fusion(bf16[6,128,512,1]{2,1,3,0:T(8,128)(2,1)S(1)} %bitcast.13, bf16[6,12,128,512]{3,2,1,0:T(8,128)(2,1)} %bitcast.12, pred[6,12]{1,0:T(8,128)(4,1)S(1)} %get-tuple-element.5), kind=kOutput, calls=%fused_computation.7 | convolution fusion | flops 1213857792 | bytes 12582984 | tf_op jit(solution)/shard_map/rik,rnjk->rnij/dot_general | solution.py:41
  79.9 0.0 all-reduce.2.cloned.1.call-update
  80.0 59.2 %all-reduce.2.cloned.1.call-done = bf16[6,12,128,128]{2,3,1,0:T(8,128)(2,1)} async-done(((bf16[6,12,128,128]{2,3,1,0:T(8,128)(2,1)}), bf16[6,12,128,128]{2,3,1,0:T(8,128)(2,1)}) %all-reduce.2.cloned.1.call-update) | async-done | bytes 2359312 | tf_op jit(solution)/shard_map/psum | solution.py:42
  139.1 1.1 convert_convert_fusion
  140.3 1.1 copy.6
  (2 shorter events, 0.0 us)
Async XLA Ops:
  6.5 42.7 %copy-start = (bf16[768,512]{1,0:T(8,128)(2,1)S(1)}, bf16[768,512]{1,0:T(8,128)(2,1)}, u32[]{:S(2)}) copy-start(bf16[768,512]{1,0:T(8,128)(2,1)} %param.4) | copy-start | bytes 2359300
  6.5 132.6 %all-reduce.2.cloned.1.call-start = ((), (), s32[]{:S(2)}) async-start(), calls=%async_computation | async-start | bytes 4718592 | tf_op jit(solution)/shard_map/psum | solution.py:42
  6.5 23.8 %collective-permute-start = (bf16[768,512]{1,0:T(8,128)(2,1)}, bf16[768,512]{1,0:T(8,128)(2,1)}, u32[]{:S(2)}, u32[]{:S(2)}) collective-permute-start(bf16[768,512]{1,0:T(8,128)(2,1)} %param.4), channel_id=1, source_target_pairs={{0,8},{4,12},{8,16},{12,20},{16,24},{20,28},{24,0},{28,4},{1,9},{5... | collective-permute-start | bytes 2359304 | tf_op jit(solution)/shard_map/ppermute | solution.py:13
  9.6 38.7 %collective-permute-start.1 = (bf16[768,512]{1,0:T(8,128)(2,1)}, bf16[768,512]{1,0:T(8,128)(2,1)S(1)}, u32[]{:S(2)}, u32[]{:S(2)}) collective-permute-start(bf16[768,512]{1,0:T(8,128)(2,1)} %param.4), channel_id=1, source_target_pairs={{0,4},{4,8},{8,12},{12,16},{16,20},{20,24},{24,28},{28,0},{1,5},{5... | collective-permute-start | bytes 2359304 | tf_op jit(solution)/shard_map/ppermute | solution.py:13
  11.1 39.1 %collective-permute-start.2 = (bf16[768,512]{1,0:T(8,128)(2,1)}, bf16[768,512]{1,0:T(8,128)(2,1)S(1)}, u32[]{:S(2)}, u32[]{:S(2)}) collective-permute-start(bf16[768,512]{1,0:T(8,128)(2,1)} %param.4), channel_id=1, source_target_pairs={{0,28},{4,0},{8,4},{12,8},{16,12},{20,16},{24,20},{28,24},{1,29},{... | collective-permute-start | bytes 2359304 | tf_op jit(solution)/shard_map/ppermute | solution.py:13
  14.3 48.8 %collective-permute-start.3 = (bf16[768,512]{1,0:T(8,128)(2,1)}, bf16[768,512]{1,0:T(8,128)(2,1)S(1)}, u32[]{:S(2)}, u32[]{:S(2)}) collective-permute-start(bf16[768,512]{1,0:T(8,128)(2,1)} %param.4), channel_id=1, source_target_pairs={{0,24},{4,28},{8,0},{12,4},{16,8},{20,12},{24,16},{28,20},{1,25},{... | collective-permute-start | bytes 2359304 | tf_op jit(solution)/shard_map/ppermute | solution.py:13
  64.1 8.1 %copy-start.1 = (bf16[768,512]{1,0:T(8,128)(2,1)S(1)}, bf16[768,512]{1,0:T(8,128)(2,1)}, u32[]{:S(2)}) copy-start(bf16[768,512]{1,0:T(8,128)(2,1)} %multiply_convert_fusion) | copy-start | bytes 2359300
Sparse Core Ops, SparseCore 0:
  80.1 59.0 all-reduce.1
where the time goes:
time: 149 us; the launch traced here: 148 us
  waiting for transfers between devices  97.9 us (66%)
  local copies, waits for them, and re-layouts  15.1 us (10%)
  between operations  13.4 us (9%)
  starting transfers between devices  8.04 us (5%)
  matrix products  7.74 us (5%)
  other arithmetic  5.92 us (4%)
    psum x1, waiting for transfers between devices, per_device(): lax.psum(partial_blocks.astype(jnp.bfloat16), 'narrow').astype(jnp.float32)  59.2 us
    ppermute x4, waiting for transfers between devices, from_behind(): return lax.ppermute(value, axis, pairs)  38.7 us
    gather x1, local copies, waits for them, and re-layouts, per_device(): jnp.take(window, local_index.reshape(-1), axis=0)  8.11 us
    ppermute x4, starting transfers between devices, from_behind(): return lax.ppermute(value, axis, pairs)  8.03 us
    dot_general x1, matrix products, per_device(): jnp.einsum('rik,rnjk->rnij', left, right, preferred_element_type=jnp.floa...  7.74 us
    unnamed x8, local copies, waits for them, and re-layouts  4.9 us
  transfers between devices with their start and end apart: 5, of which 4 were waited for; matrix products, arithmetic and copies ran while one was open for 7% of the time, Pallas kernels for 0%

commit v1 on v0

v1 whole, which is shorter than its diff:
```python
import functools

import jax
import jax.numpy as jnp
from jax import lax
from jax.experimental import pallas as pl
from jax.experimental.pallas import tpu as pltpu
from jax.sharding import PartitionSpec as P

B = 128
REACH = 8
CL = 6
PAIR = 2
VMEM = pl.BlockSpec(memory_space=pltpu.VMEM)
SMEM = pl.BlockSpec(memory_space=pltpu.SMEM)
LIMIT = 40 * 1024 * 1024
SHORT = pl.CostEstimate(flops=1, bytes_accessed=1, transcendentals=0)


def move(value, axis, target):
    count = lax.axis_size(axis)
    return lax.ppermute(value, axis, [(s, target(s) % count) for s in range(count)])


def outward(w):
    return w + 2 if w % 2 == 0 else w - 2


def inward(w):
    return w - 2 if w % 2 == 0 else w + 2


def blocks_kernel(clusters, share, marks, first, last, pattern, left, own, after, *refs):
    pieces = refs[: len(marks)]
    outs = refs[len(marks) : len(marks) + 4]
    dense = refs[len(marks) + 4]
    wide = lax.axis_index("wide")
    me = lax.axis_index("narrow")
    odd = lax.rem(wide, 2)

    def natural(low, high):
        return jnp.where(odd == 1, low, CL - 1 - high)

    def multiply(rows, offset, c0, c1):
        count = c1 - c0 + 1
        start = natural(c0, c1)
        product = lax.dot_general(
            left[pl.ds(pl.multiple_of(start * B, B), count * B), :],
            rows,
            (((1,), (1,)), ((), ())),
            preferred_element_type=jnp.float32,
        ).astype(jnp.bfloat16)
        for r in range(count):
            for h in range(PAIR):
                dense[start + r, offset + REACH + h] = product[r * B : (r + 1) * B, h * B : (h + 1) * B]

    for offset in range(0, CL, PAIR):
        multiply(own[offset * B : (offset + PAIR) * B, :], offset, first, last)
    for piece, mark in zip(pieces, marks):
        c0, c1 = max(first, mark - REACH), min(last, mark + PAIR - 1 + REACH)
        multiply(piece[...], natural(mark, mark + PAIR - 1), c0, c1)

    base = wide * CL - REACH
    start = natural(first, last)
    for out, mask in zip(outs, (3, 1, 2, 0)):
        slot0 = (me ^ mask) * share
        for r in range(last - first + 1):
            for s in range(share):
                where = lax.rem(pattern[start + r, slot0 + s] - base + clusters, clusters)
                out[r, s] = dense[start + r, where]


def blocks(clusters, share, first, last, pattern, left, own, window, after):
    marks = [m for m in window if m + PAIR - 1 >= first - REACH and m <= last + REACH]
    shape = jax.ShapeDtypeStruct((last - first + 1, share, B, B), jnp.bfloat16)
    return pl.pallas_call(
        functools.partial(blocks_kernel, clusters, share, marks, first, last),
        out_shape=[shape] * 4,
        in_specs=[SMEM, VMEM, VMEM, pl.BlockSpec(memory_space=pl.ANY)] + [VMEM] * len(marks),
        out_specs=[VMEM] * 4,
        scratch_shapes=[pltpu.VMEM((CL, CL + 2 * REACH, B, B), jnp.bfloat16)],
        compiler_params=pltpu.CompilerParams(vmem_limit_bytes=LIMIT),
        cost_estimate=SHORT,
        name=f"blocks_{first}_{last}",
    )(pattern, left, own, after, *[window[m] for m in marks])


def finish_kernel(chunks, *refs):
    out = refs[-1]
    odd = lax.rem(lax.axis_index("wide"), 2)
    for at, (first, last) in enumerate(chunks):
        near, got_near, got = refs[3 * at : 3 * at + 3]
        start = jnp.where(odd == 1, first, CL - 1 - last)
        for r in range(last - first + 1):
            total = near[r].astype(jnp.float32) + got_near[r].astype(jnp.float32) + got[r].astype(jnp.float32)
            out[start + r] = total.astype(jnp.bfloat16)


def per_device(slab, occupation, column_band, pattern):
    clusters = CL * lax.axis_size("wide")
    share = pattern.shape[1] // lax.axis_size("narrow")
    odd = lax.axis_index("wide") % 2
    rows = PAIR * B
    partner = lambda w: w ^ 1

    far_rows = lax.dynamic_slice_in_dim(slab, odd * 2 * rows, rows, 0)
    near_rows = lax.dynamic_slice_in_dim(slab, (1 - odd) * 2 * rows, rows, 0)
    middle_rows = slab[rows : 2 * rows]
    window = {}
    window[-6] = move(far_rows, "wide", partner)
    window[-4] = move(middle_rows, "wide", partner)
    window[-2] = move(near_rows, "wide", partner)
    window[-8] = move(far_rows, "wide", inward)
    window[12] = move(near_rows, "wide", outward)
    window[6] = move(window[-6], "wide", outward)
    window[8] = move(window[-4], "wide", outward)
    window[10] = move(window[-2], "wide", outward)

    picks = column_band[:, None] == jnp.arange(occupation.shape[0], dtype=jnp.int32)[None, :]
    weight = jnp.sum(jnp.where(picks, occupation[None, :], jnp.float32(0.0)), axis=1)
    scaled = (slab.astype(jnp.float32) * weight[None, :]).astype(jnp.bfloat16)

    chunks = ((0, 1), (2, 5))
    parts = []
    far = pattern
    for first, last in chunks:
        send_far, send_near, keep_far, keep_near = blocks(
            clusters, share, first, last, pattern, scaled, slab, window, far
        )
        got_far = move(send_far, "narrow", lambda n: n ^ 1)
        got_near = move(send_near, "narrow", lambda n: n ^ 1)
        far = (keep_far.astype(jnp.float32) + got_far.astype(jnp.float32)).astype(jnp.bfloat16)
        parts += [keep_near, got_near, move(far, "narrow", lambda n: n ^ 2)]
    return pl.pallas_call(
        functools.partial(finish_kernel, chunks),
        out_shape=jax.ShapeDtypeStruct((CL, share, B, B), jnp.bfloat16),
        in_specs=[VMEM] * len(parts),
        out_specs=VMEM,
        compiler_params=pltpu.CompilerParams(vmem_limit_bytes=LIMIT),
        cost_estimate=SHORT,
        name="finish",
    )(*parts)


def solution(mesh):
    placed = (P("wide", "narrow"), P(), P("narrow"), P("wide", None))
    return jax.shard_map(
        per_device,
        mesh=mesh,
        in_specs=placed,
        out_specs=P("wide", "narrow", None, None),
        check_vma=False,
    )
```

time: 149 us -> 72.3 us (0.49)
  waiting for transfers between devices: 97.9 us -> 54.1 us
  local copies, waits for them, and re-layouts: 15.1 us -> 1.25 us
  between operations: 13.4 us -> 0.09 us
  matrix products: 7.74 us -> 0 us
  Pallas kernels: 0 us -> 4.62 us
  other arithmetic: 5.92 us -> 1.54 us
  starting transfers between devices: 8.04 us -> 10.6 us
    psum x1 -> x0, waiting for transfers between devices: 59.2 us -> none  [per_device(): lax.psum(partial_blocks.astype(jnp.bfloat16), 'narrow').astype(jnp.float32)]
    ppermute x4 -> x14, waiting for transfers between devices: 38.7 us -> 54.1 us  [move(): lax.ppermute(value, axis, [(s, target(s) % count) for s in range(count)])]
    gather x1 -> x0, local copies, waits for them, and re-layouts: 8.11 us -> none  [per_device(): jnp.take(window, local_index.reshape(-1), axis=0)]
    dot_general x1 -> x0, matrix products: 7.74 us -> none  [per_device(): jnp.einsum('rik,rnjk->rnij', left, right, preferred_element_type=jnp.floa...]
    unnamed x8, local copies, waits for them, and re-layouts: 4.9 us -> 0.02 us
    pallas_call x0 -> x3, Pallas kernels: none -> 4.62 us  [the longest x2 3.6 us: blocks(): pl.pallas_call(functools.partial(blocks_kernel, clusters, share, marks, f...]
    ppermute x4 -> x14, starting transfers between devices: 8.03 us -> 10.6 us  [move(): lax.ppermute(value, axis, [(s, target(s) % count) for s in range(count)])]
    convert_element_type x1, other arithmetic: 2.15 us -> 0.16 us  [per_device(): scaled = (slab.astype(jnp.float32) * weight[None, :]).astype(jnp.bfloat16)]
  transfers between devices with their start and end apart: 5 -> 14, of which waited for: 4 -> 10; matrix products, arithmetic and copies ran while one was open for 7% -> 2% of each run, Pallas kernels for 0% -> 0%
where the time goes in v1:
time: 72.3 us; the launch traced here: 72.2 us
  waiting for transfers between devices  54.1 us (75%)
  starting transfers between devices  10.6 us (15%)
  Pallas kernels  4.62 us (6%)
  other arithmetic  1.54 us (2%)
  local copies, waits for them, and re-layouts  1.25 us (2%)
    ppermute x14, waiting for transfers between devices, move(): lax.ppermute(value, axis, [(s, target(s) % count) for s in range(count)])  54.1 us
    ppermute x14, starting transfers between devices, move(): lax.ppermute(value, axis, [(s, target(s) % count) for s in range(count)])  10.6 us
    pallas_call x2, Pallas kernels, blocks(): pl.pallas_call(functools.partial(blocks_kernel, clusters, share, marks, f...  3.6 us
  transfers between devices with their start and end apart: 14, of which 10 were waited for; matrix products, arithmetic and copies ran while one was open for 2% of the time, Pallas kernels for 0%

profile of v1, /device:TPU:0, one launch (start us, length us, event | category | flops | bytes accessed | tf_op | source)
XLA Modules:
  0.0 72.2 jit_solution(16195932424268339362)
XLA Ops:
  0.0 0.0 copy-start.2
  0.0 0.0 copy-start.3
  0.0 0.0 copy-start
  0.0 1.2 %constant_dynamic-slice_fusion = (bf16[256,512]{1,0:T(8,128)(2,1)S(1)}, bf16[256,512]{1,0:T(8,128)(2,1)S(1)}, bf16[256,512]{1,0:T(8,128)(2,1)S(1)}) fusion(bf16[768,512]{1,0:T(8,128)(2,1)} %own.3, s32[]{:T(128)S(6)} %select_n.20, s32[]{:T(128)S(6)} %select_n.19), kind=kLoop, calls=%fused_computation.5 | loop fusion | bytes 1572872 | tf_op jit(solution)/shard_map/dynamic_slice | solution.py:107
  1.2 5.1 %collective-permute-start.3 = (bf16[256,512]{1,0:T(8,128)(2,1)S(1)}, bf16[256,512]{1,0:T(8,128)(2,1)S(1)}, u32[]{:S(2)}, u32[]{:S(2)}) collective-permute-start(bf16[256,512]{1,0:T(8,128)(2,1)S(1)} %get-tuple-element.23), channel_id=1, source_target_pairs={{0,24},{4,12},{8,0},{12,20},{16,8},{20,28},{24,16},{28,4},{1,25},{... | collective-permute-start | bytes 786440 | tf_op jit(solution)/shard_map/ppermute | solution.py:22
  6.4 0.0 collective-permute-start
  6.4 2.0 %collective-permute-start.1 = (bf16[256,512]{1,0:T(8,128)(2,1)S(1)}, bf16[256,512]{1,0:T(8,128)(2,1)S(1)}, u32[]{:S(2)}, u32[]{:S(2)}) collective-permute-start(bf16[256,512]{1,0:T(8,128)(2,1)S(1)} %get-tuple-element.22), channel_id=1, source_target_pairs={{0,4},{4,0},{8,12},{12,8},{16,20},{20,16},{24,28},{28,24},{1,5},{5... | collective-permute-start | bytes 786440 | tf_op jit(solution)/shard_map/ppermute | solution.py:22
  8.4 0.0 collective-permute-start.2
  8.4 0.0 copy-done.2
  8.4 0.0 copy-done.3
  8.4 1.2 %select_reduce_fusion = f32[512]{0:T(512)S(1)} fusion(f32[4096]{0:T(1024)S(1)} %copy-done.2, s32[512]{0:T(512)S(1)} %copy-done.3), kind=kLoop, calls=%fused_computation | loop fusion | flops 6290944 | bytes 20480 | tf_op jit(solution)/shard_map/reduce_sum | solution.py:120
  9.7 0.0 copy-start.1
  9.7 11.5 %collective-permute-done.1.refs_1_ = bf16[256,512]{1,0:T(8,128)(2,1)S(1)} collective-permute-done((bf16[256,512]{1,0:T(8,128)(2,1)S(1)}, bf16[256,512]{1,0:T(8,128)(2,1)S(1)}, u32[]{:S(2)}, u32[]{:S(2)}) %collective-permute-start.1) | collective-permute-done | bytes 262176 | tf_op jit(solution)/shard_map/ppermute | solution.py:22
  21.2 0.0 collective-permute-start.5
  21.2 0.0 collective-permute-done.refs_0_
  21.2 0.6 collective-permute-start.4
  21.8 0.0 copy-done
  21.8 0.2 multiply_convert_fusion.left
  22.0 3.4 %collective-permute-done.2.refs_2_ = bf16[256,512]{1,0:T(8,128)(2,1)S(1)} collective-permute-done((bf16[256,512]{1,0:T(8,128)(2,1)S(1)}, bf16[256,512]{1,0:T(8,128)(2,1)S(1)}, u32[]{:S(2)}, u32[]{:S(2)}) %collective-permute-start.2) | collective-permute-done | bytes 262176 | tf_op jit(solution)/shard_map/ppermute | solution.py:22
  25.4 0.0 collective-permute-done.3.refs_3_
  25.4 5.8 %collective-permute-done.5.refs_5_ = bf16[256,512]{1,0:T(8,128)(2,1)S(1)} collective-permute-done((bf16[256,512]{1,0:T(8,128)(2,1)S(1)}, bf16[256,512]{1,0:T(8,128)(2,1)S(1)}, u32[]{:S(2)}, u32[]{:S(2)}) %collective-permute-start.5) | collective-permute-done | bytes 262176 | tf_op jit(solution)/shard_map/ppermute | solution.py:22
  31.2 2.8 %collective-permute-done.4.refs_4_ = bf16[256,512]{1,0:T(8,128)(2,1)S(1)} collective-permute-done((bf16[256,512]{1,0:T(8,128)(2,1)S(1)}, bf16[256,512]{1,0:T(8,128)(2,1)S(1)}, u32[]{:S(2)}, u32[]{:S(2)}) %collective-permute-start.4) | collective-permute-done | bytes 262176 | tf_op jit(solution)/shard_map/ppermute | solution.py:22
  34.0 0.0 copy-done.1
  34.0 1.5 %blocks_0_1.1 = (bf16[2,3,128,128]{3,2,1,0:T(8,128)(2,1)S(1)}, bf16[2,3,128,128]{3,2,1,0:T(8,128)(2,1)S(1)}, bf16[2,3,128,128]{3,2,1,0:T(8,128)(2,1)S(1)}, bf16[2,3,128,128]{3,2,1,0:T(8,128)(2,1)S(1)}) custom-call(s32[6,12]{1,0:T(8,128)S(1)} %copy-done.1, bf16[768,512]{1,0:T(8,128)(2,1)S(1)} %multiply_convert_fusion.left, bf16[768,512]{1,0:T(8,128)(2,1)S(1)} %copy-done, ...), custom_call_target="tpu_custom_call" | custom-call | flops 1 | bytes 1 | tf_op jit(solution)/shard_map/blocks_0_1/pallas_call | solution.py:76
  35.5 0.1 collective-permute-start.7
  35.6 0.1 collective-permute-start.9
  35.6 0.1 collective-permute-start.10
  35.7 1.3 %collective-permute-done.7 = bf16[2,3,128,128]{3,2,1,0:T(8,128)(2,1)S(1)} collective-permute-done((bf16[2,3,128,128]{3,2,1,0:T(8,128)(2,1)S(1)}, bf16[2,3,128,128]{3,2,1,0:T(8,128)(2,1)S(1)}, u32[]{:S(2)}, u32[]{:S(2)}) %collective-permute-start.7) | collective-permute-done | bytes 196640 | tf_op jit(solution)/shard_map/ppermute | solution.py:22
  37.0 0.1 add_convert_fusion.1.after
  37.1 9.5 %collective-permute-done.9.refs_3_ = bf16[256,512]{1,0:T(8,128)(2,1)S(1)} collective-permute-done((bf16[256,512]{1,0:T(8,128)(2,1)S(1)}, bf16[256,512]{1,0:T(8,128)(2,1)S(1)}, u32[]{:S(2)}, u32[]{:S(2)}) %collective-permute-start.9) | collective-permute-done | bytes 262176 | tf_op jit(solution)/shard_map/ppermute | solution.py:22
  46.5 5.2 %collective-permute-done.10.refs_6_ = bf16[256,512]{1,0:T(8,128)(2,1)S(1)} collective-permute-done((bf16[256,512]{1,0:T(8,128)(2,1)S(1)}, bf16[256,512]{1,0:T(8,128)(2,1)S(1)}, u32[]{:S(2)}, u32[]{:S(2)}) %collective-permute-start.10) | collective-permute-done | bytes 262176 | tf_op jit(solution)/shard_map/ppermute | solution.py:22
  51.7 2.1 %blocks_2_5.1 = (bf16[4,3,128,128]{3,2,1,0:T(8,128)(2,1)S(1)}, bf16[4,3,128,128]{3,2,1,0:T(8,128)(2,1)S(1)}, bf16[4,3,128,128]{3,2,1,0:T(8,128)(2,1)S(1)}, bf16[4,3,128,128]{3,2,1,0:T(8,128)(2,1)S(1)}) custom-call(s32[6,12]{1,0:T(8,128)S(1)} %copy-done.1, bf16[768,512]{1,0:T(8,128)(2,1)S(1)} %multiply_convert_fusion.left, bf16[768,512]{1,0:T(8,128)(2,1)S(1)} %copy-done, ...), custom_call_target="tpu_custom_call" | custom-call | flops 1 | bytes 1 | tf_op jit(solution)/shard_map/blocks_2_5/pallas_call | solution.py:76
  53.8 0.1 collective-permute-start.12
  53.9 0.5 collective-permute-start.11
  54.4 1.2 %collective-permute-done.12 = bf16[4,3,128,128]{3,2,1,0:T(8,128)(2,1)S(1)} collective-permute-done((bf16[4,3,128,128]{3,2,1,0:T(8,128)(2,1)S(1)}, bf16[4,3,128,128]{3,2,1,0:T(8,128)(2,1)S(1)}, u32[]{:S(2)}, u32[]{:S(2)}) %collective-permute-start.12) | collective-permute-done | bytes 393248 | tf_op jit(solution)/shard_map/ppermute | solution.py:22
  55.6 0.1 add_convert_fusion
  55.7 1.6 %collective-permute-start.13 = (bf16[4,3,128,128]{3,2,1,0:T(8,128)(2,1)S(1)}, bf16[4,3,128,128]{3,2,1,0:T(8,128)(2,1)S(1)}, u32[]{:S(2)}, u32[]{:S(2)}) collective-permute-start(bf16[4,3,128,128]{3,2,1,0:T(8,128)(2,1)S(1)} %add_convert_fusion), channel_id=1, source_target_pairs={{0,2},{1,3},{2,0},{3,1},{4,6},{5,7},{6,4},{7,5},{8,10},{9,11},{10,... | collective-permute-start | bytes 1179656 | tf_op jit(solution)/shard_map/ppermute | solution.py:22
  57.3 0.0 collective-permute-start.6
  57.3 0.5 collective-permute-start.8
  57.8 0.9 %collective-permute-done.6.refs_1_ = bf16[2,3,128,128]{3,2,1,0:T(8,128)(2,1)S(1)} collective-permute-done((bf16[2,3,128,128]{3,2,1,0:T(8,128)(2,1)S(1)}, bf16[2,3,128,128]{3,2,1,0:T(8,128)(2,1)S(1)}, u32[]{:S(2)}, u32[]{:S(2)}) %collective-permute-start.6) | collective-permute-done | bytes 196640 | tf_op jit(solution)/shard_map/ppermute | solution.py:22
  58.7 12.4 %collective-permute-done.8.refs_2_ = bf16[2,3,128,128]{3,2,1,0:T(8,128)(2,1)S(1)} collective-permute-done((bf16[2,3,128,128]{3,2,1,0:T(8,128)(2,1)S(1)}, bf16[2,3,128,128]{3,2,1,0:T(8,128)(2,1)S(1)}, u32[]{:S(2)}, u32[]{:S(2)}) %collective-permute-start.8) | collective-permute-done | bytes 196640 | tf_op jit(solution)/shard_map/ppermute | solution.py:22
  71.2 0.0 collective-permute-done.11.refs_4_
  71.2 0.0 collective-permute-done.13.refs_5_
  71.2 1.0 %finish.1 = bf16[6,3,128,128]{3,2,1,0:T(8,128)(2,1)} custom-call(bf16[2,3,128,128]{3,2,1,0:T(8,128)(2,1)S(1)} %get-tuple-element.13.refs_0_, bf16[2,3,128,128]{3,2,1,0:T(8,128)(2,1)S(1)} %collective-permute-done.6.refs_1_, bf16[2,3,128,128]{3,2,1,0:T(8,128)(2,1)S(1)} %collective-permute-done.8.refs_2_, ...), custom_call_target="tpu_custom_call" | custom-call | flops 1 | bytes 1 | tf_op jit(solution)/shard_map/finish/pallas_call | solution.py:134
Async XLA Ops:
  0.0 8.4 %copy-start.2 = (f32[4096]{0:T(1024)S(1)}, f32[4096]{0:T(1024)}, u32[]{:S(2)}) copy-start(f32[4096]{0:T(1024)} %param.5) | copy-start | bytes 49156
  0.0 8.4 %copy-start.3 = (s32[512]{0:T(512)S(1)}, s32[512]{0:T(512)}, u32[]{:S(2)}) copy-start(s32[512]{0:T(512)} %param.6) | copy-start | bytes 6148
  0.0 21.8 %copy-start = (bf16[768,512]{1,0:T(8,128)(2,1)S(1)}, bf16[768,512]{1,0:T(8,128)(2,1)}, u32[]{:S(2)}) copy-start(bf16[768,512]{1,0:T(8,128)(2,1)} %own.3) | copy-start | bytes 2359300
  1.2 24.1 %collective-permute-start.3 = (bf16[256,512]{1,0:T(8,128)(2,1)S(1)}, bf16[256,512]{1,0:T(8,128)(2,1)S(1)}, u32[]{:S(2)}, u32[]{:S(2)}) collective-permute-start(bf16[256,512]{1,0:T(8,128)(2,1)S(1)} %get-tuple-element.23), channel_id=1, source_target_pairs={{0,24},{4,12},{8,0},{12,20},{16,8},{20,28},{24,16},{28,4},{1,25},{... | collective-permute-start | bytes 786440 | tf_op jit(solution)/shard_map/ppermute | solution.py:22
  6.4 14.9 %collective-permute-start = (bf16[256,512]{1,0:T(8,128)(2,1)S(1)}, bf16[256,512]{1,0:T(8,128)(2,1)S(1)}, u32[]{:S(2)}, u32[]{:S(2)}) collective-permute-start(bf16[256,512]{1,0:T(8,128)(2,1)S(1)} %get-tuple-element.23), channel_id=1, source_target_pairs={{0,4},{4,0},{8,12},{12,8},{16,20},{20,16},{24,28},{28,24},{1,5},{5... | collective-permute-start | bytes 786440 | tf_op jit(solution)/shard_map/ppermute | solution.py:22
  6.4 14.8 %collective-permute-start.1 = (bf16[256,512]{1,0:T(8,128)(2,1)S(1)}, bf16[256,512]{1,0:T(8,128)(2,1)S(1)}, u32[]{:S(2)}, u32[]{:S(2)}) collective-permute-start(bf16[256,512]{1,0:T(8,128)(2,1)S(1)} %get-tuple-element.22), channel_id=1, source_target_pairs={{0,4},{4,0},{8,12},{12,8},{16,20},{20,16},{24,28},{28,24},{1,5},{5... | collective-permute-start | bytes 786440 | tf_op jit(solution)/shard_map/ppermute | solution.py:22
  8.4 17.0 %collective-permute-start.2 = (bf16[256,512]{1,0:T(8,128)(2,1)S(1)}, bf16[256,512]{1,0:T(8,128)(2,1)S(1)}, u32[]{:S(2)}, u32[]{:S(2)}) collective-permute-start(bf16[256,512]{1,0:T(8,128)(2,1)S(1)} %get-tuple-element.21), channel_id=1, source_target_pairs={{0,4},{4,0},{8,12},{12,8},{16,20},{20,16},{24,28},{28,24},{1,5},{5... | collective-permute-start | bytes 786440 | tf_op jit(solution)/shard_map/ppermute | solution.py:22
  9.7 24.4 %copy-start.1 = (s32[6,12]{1,0:T(8,128)S(1)}, s32[6,12]{1,0:T(8,128)}, u32[]{:S(2)}) copy-start(s32[6,12]{1,0:T(8,128)} %pattern.3) | copy-start | bytes 868
  21.2 10.0 %collective-permute-start.5 = (bf16[256,512]{1,0:T(8,128)(2,1)S(1)}, bf16[256,512]{1,0:T(8,128)(2,1)S(1)}, u32[]{:S(2)}, u32[]{:S(2)}) collective-permute-start(bf16[256,512]{1,0:T(8,128)(2,1)S(1)} %collective-permute-done.1.refs_1_), channel_id=1, source_target_pairs={{0,8},{4,28},{8,16},{12,4},{16,24},{20,12},{24,0},{28,20},{1,9},{5... | collective-permute-start | bytes 786440 | tf_op jit(solution)/shard_map/ppermute | solution.py:22
  21.2 12.8 %collective-permute-start.4 = (bf16[256,512]{1,0:T(8,128)(2,1)S(1)}, bf16[256,512]{1,0:T(8,128)(2,1)S(1)}, u32[]{:S(2)}, u32[]{:S(2)}) collective-permute-start(bf16[256,512]{1,0:T(8,128)(2,1)S(1)} %collective-permute-done.refs_0_), channel_id=1, source_target_pairs={{0,8},{4,28},{8,16},{12,4},{16,24},{20,12},{24,0},{28,20},{1,9},{5... | collective-permute-start | bytes 786440 | tf_op jit(solution)/shard_map/ppermute | solution.py:22
  35.5 1.5 %collective-permute-start.7 = (bf16[2,3,128,128]{3,2,1,0:T(8,128)(2,1)S(1)}, bf16[2,3,128,128]{3,2,1,0:T(8,128)(2,1)S(1)}, u32[]{:S(2)}, u32[]{:S(2)}) collective-permute-start(bf16[2,3,128,128]{3,2,1,0:T(8,128)(2,1)S(1)} %get-tuple-element.16), channel_id=1, source_target_pairs={{0,1},{1,0},{2,3},{3,2},{4,5},{5,4},{6,7},{7,6},{8,9},{9,8},{10,11... | collective-permute-start | bytes 589832 | tf_op jit(solution)/shard_map/ppermute | solution.py:22
  35.6 11.0 %collective-permute-start.9 = (bf16[256,512]{1,0:T(8,128)(2,1)S(1)}, bf16[256,512]{1,0:T(8,128)(2,1)S(1)}, u32[]{:S(2)}, u32[]{:S(2)}) collective-permute-start(bf16[256,512]{1,0:T(8,128)(2,1)S(1)} %get-tuple-element.21), channel_id=1, source_target_pairs={{0,8},{4,28},{8,16},{12,4},{16,24},{20,12},{24,0},{28,20},{1,9},{5... | collective-permute-start | bytes 786440 | tf_op jit(solution)/shard_map/ppermute | solution.py:22
  35.6 16.1 %collective-permute-start.10 = (bf16[256,512]{1,0:T(8,128)(2,1)S(1)}, bf16[256,512]{1,0:T(8,128)(2,1)S(1)}, u32[]{:S(2)}, u32[]{:S(2)}) collective-permute-start(bf16[256,512]{1,0:T(8,128)(2,1)S(1)} %collective-permute-done.2.refs_2_), channel_id=1, source_target_pairs={{0,8},{4,28},{8,16},{12,4},{16,24},{20,12},{24,0},{28,20},{1,9},{5... | collective-permute-start | bytes 786440 | tf_op jit(solution)/shard_map/ppermute | solution.py:22
  53.8 1.8 %collective-permute-start.12 = (bf16[4,3,128,128]{3,2,1,0:T(8,128)(2,1)S(1)}, bf16[4,3,128,128]{3,2,1,0:T(8,128)(2,1)S(1)}, u32[]{:S(2)}, u32[]{:S(2)}) collective-permute-start(bf16[4,3,128,128]{3,2,1,0:T(8,128)(2,1)S(1)} %get-tuple-element.20), channel_id=1, source_target_pairs={{0,1},{1,0},{2,3},{3,2},{4,5},{5,4},{6,7},{7,6},{8,9},{9,8},{10,11... | collective-permute-start | bytes 1179656 | tf_op jit(solution)/shard_map/ppermute | solution.py:22
  53.9 17.3 %collective-permute-start.11 = (bf16[4,3,128,128]{3,2,1,0:T(8,128)(2,1)S(1)}, bf16[4,3,128,128]{3,2,1,0:T(8,128)(2,1)S(1)}, u32[]{:S(2)}, u32[]{:S(2)}) collective-permute-start(bf16[4,3,128,128]{3,2,1,0:T(8,128)(2,1)S(1)} %get-tuple-element.18), channel_id=1, source_target_pairs={{0,1},{1,0},{2,3},{3,2},{4,5},{5,4},{6,7},{7,6},{8,9},{9,8},{10,11... | collective-permute-start | bytes 1179656 | tf_op jit(solution)/shard_map/ppermute | solution.py:22
  55.7 15.4 %collective-permute-start.13 = (bf16[4,3,128,128]{3,2,1,0:T(8,128)(2,1)S(1)}, bf16[4,3,128,128]{3,2,1,0:T(8,128)(2,1)S(1)}, u32[]{:S(2)}, u32[]{:S(2)}) collective-permute-start(bf16[4,3,128,128]{3,2,1,0:T(8,128)(2,1)S(1)} %add_convert_fusion), channel_id=1, source_target_pairs={{0,2},{1,3},{2,0},{3,1},{4,6},{5,7},{6,4},{7,5},{8,10},{9,11},{10,... | collective-permute-start | bytes 1179656 | tf_op jit(solution)/shard_map/ppermute | solution.py:22
  57.3 1.4 %collective-permute-start.6 = (bf16[2,3,128,128]{3,2,1,0:T(8,128)(2,1)S(1)}, bf16[2,3,128,128]{3,2,1,0:T(8,128)(2,1)S(1)}, u32[]{:S(2)}, u32[]{:S(2)}) collective-permute-start(bf16[2,3,128,128]{3,2,1,0:T(8,128)(2,1)S(1)} %get-tuple-element.14), channel_id=1, source_target_pairs={{0,1},{1,0},{2,3},{3,2},{4,5},{5,4},{6,7},{7,6},{8,9},{9,8},{10,11... | collective-permute-start | bytes 589832 | tf_op jit(solution)/shard_map/ppermute | solution.py:22
  57.3 13.9 %collective-permute-start.8 = (bf16[2,3,128,128]{3,2,1,0:T(8,128)(2,1)S(1)}, bf16[2,3,128,128]{3,2,1,0:T(8,128)(2,1)S(1)}, u32[]{:S(2)}, u32[]{:S(2)}) collective-permute-start(bf16[2,3,128,128]{3,2,1,0:T(8,128)(2,1)S(1)} %add_convert_fusion.1.after), channel_id=1, source_target_pairs={{0,2},{1,3},{2,0},{3,1},{4,6},{5,7},{6,4},{7,5},{8,10},{9,11},{10,... | collective-permute-start | bytes 589832 | tf_op jit(solution)/shard_map/ppermute | solution.py:22
